TPU v7x, 32 devices: a whole 2x2x4 slice. The times are simulated.
32 devices in a mesh: group: 2 (over y), dp: 16 (over z, x, core).
Axes of the slice: x: 2, y: 2, z: 4, core: 2. Of those that a mesh axis runs over, the one named last changes fastest.
Arguments:
- tokens: bfloat16 [4096, 8192], P(('group', 'dp')), parts along dimension 0, may hold values from -6 to 6
- output_cotangent: bfloat16 [4096, 512], P(('group', 'dp')), parts along dimension 0, may hold values from -6 to 6
- frozen_value_weight: bfloat16 [8192, 512], P('dp'), may hold values from -0.0625 to 0.0625
- adapter_lowering: bfloat16 [256, 16, 8192], P(('group', 'dp')), parts along dimension 0, may hold values from -0.0625 to 0.0625
- adapter_raising: bfloat16 [256, 16, 512], P(('group', 'dp')), parts along dimension 0, may hold values from -0.25 to 0.25
- tenant: int32 [4096], P(('group', 'dp')), parts along dimension 0, may hold values from 0 to 127, as said below
- tenant_row_index: int32 [256], P('group'), parts along dimension 0, may hold values from 0 to 127, as said below
Outputs:
- projected: bfloat16 [4096, 512], P(('group', 'dp')), parts along dimension 0
- token_input_grad: bfloat16 [4096, 8192], P(('group', 'dp')), parts along dimension 0
- grad_down: bfloat16 [256, 16, 8192], P(('group', 'dp')), parts along dimension 0
- grad_up: bfloat16 [256, 16, 512], P(('group', 'dp')), parts along dimension 0
There are 2 independent parts, one for each index of `group`. A program takes and returns all parts, laid end to end along the dimension named above; an argument that names none is the same for every part. Nothing has to cross between parts.
Inputs may be any that keep to these rules, and one draw needn't show every extreme that they name: tenant[i] is the adapter of token i. The 128 tokens of device k form 4 runs of consecutive tokens, each run of one adapter; every run's adapter has its row (tenant_row_index of it) among the rows of device k - 1, k or k + 1, taken modulo 16, where device j holds rows 8 * j to 8 * j + 7. In every draw each device has runs on the rows of all three of these devices. A permutation: adapter a is row tenant_row_index[a] of adapter_lowering and adapter_raising.
All inputs are finite; a program needn't handle non-finite values.
Results may differ from a plain program's by a relative error of at most 0.0051.
Values may be sent and summed in bfloat16 or wider, within the bound.
A program may use at most 128 MiB of HBM per device.

v0:
```python
import jax
import jax.numpy as jnp
from jax import lax
from jax.sharding import PartitionSpec as P


def padded(cells, sides, width):
    for axis, dim in sides:
        count = lax.axis_size(axis)
        head = lax.slice_in_dim(cells, 0, width, axis=dim)
        tail = lax.slice_in_dim(cells, cells.shape[dim] - width, cells.shape[dim], axis=dim)
        cells = jnp.concatenate(
            [
                lax.ppermute(tail, axis, [(i, (i + 1) % count) for i in range(count)]),
                cells,
                lax.ppermute(head, axis, [((i + 1) % count, i) for i in range(count)]),
            ],
            axis=dim,
        )
    return cells


def body(
    tokens,
    output_cotangent,
    frozen_value_weight,
    adapter_lowering,
    adapter_raising,
    tenant,
    tenant_row_index,
):
    devices = lax.axis_size("dp")
    here = lax.axis_index("dp")
    model_width = tokens.shape[1]
    value_width = output_cotangent.shape[1]
    written_totals = adapter_lowering.shape[0]
    rank_feature_width = adapter_lowering.shape[1]
    contract = (((1,), (1,)), ((), ()))
    over_slots = (((0,), (0,)), ((), ()))
    row_index = jnp.take(tenant_row_index, tenant)
    owners = row_index // written_totals
    side = (owners - here + 1 + devices) % devices
    local_slot = side * written_totals + row_index % written_totals
    write_totals = jnp.concatenate([adapter_lowering, adapter_raising], axis=2)
    nearby = padded(write_totals, (("dp", 0),), written_totals)
    span = 3 * written_totals * rank_feature_width
    lowering_rows_flat = nearby[:, :, :model_width].reshape(span, model_width)
    raising_rows_flat = nearby[:, :, model_width:].reshape(span, value_width)
    column_slot = jnp.arange(span) // rank_feature_width
    select = (local_slot[:, None] == column_slot[None, :]).astype(jnp.float32)
    narrow_rank_rows = (
        lax.dot_general(tokens, lowering_rows_flat, contract, preferred_element_type=jnp.float32)
        * select
    ).astype(jnp.bfloat16)
    reverse_rank_rows = (
        lax.dot_general(
            output_cotangent, raising_rows_flat, contract, preferred_element_type=jnp.float32
        )
        * select
    ).astype(jnp.bfloat16)
    adapter_output = jnp.dot(
        narrow_rank_rows, raising_rows_flat, preferred_element_type=jnp.float32
    ).astype(jnp.bfloat16)
    adapter_input_grad = jnp.dot(
        reverse_rank_rows, lowering_rows_flat, preferred_element_type=jnp.float32
    ).astype(jnp.bfloat16)
    down_terms = lax.dot_general(
        reverse_rank_rows, tokens, over_slots, preferred_element_type=jnp.float32
    )
    up_terms = lax.dot_general(
        narrow_rank_rows, output_cotangent, over_slots, preferred_element_type=jnp.float32
    )
    partial_value = jnp.concatenate([down_terms, up_terms], axis=1).reshape(
        3 * written_totals, rank_feature_width, model_width + value_width
    )
    edges = jnp.concatenate(
        [partial_value[:written_totals], partial_value[2 * written_totals :]], axis=0
    )
    returned = padded(edges, (("dp", 0),), written_totals)
    totals = (
        partial_value[written_totals : 2 * written_totals]
        + returned[:written_totals]
        + returned[3 * written_totals :]
    )
    grad_down = totals[:, :, :model_width].astype(jnp.bfloat16)
    grad_up = totals[:, :, model_width:].astype(jnp.bfloat16)
    frozen_output = jnp.dot(
        tokens,
        lax.all_gather(frozen_value_weight, "dp", axis=0, tiled=True),
        preferred_element_type=jnp.float32,
    )
    frozen_input_grad = lax.dot_general(
        output_cotangent,
        lax.all_gather(frozen_value_weight, "dp", axis=0, tiled=True),
        contract,
        preferred_element_type=jnp.float32,
    )
    projected = (frozen_output + adapter_output.astype(jnp.float32)).astype(jnp.bfloat16)
    token_input_grad = (frozen_input_grad + adapter_input_grad.astype(jnp.float32)).astype(
        jnp.bfloat16
    )
    return (projected, token_input_grad, grad_down, grad_up)


def solution(mesh):
    placed = (
        P(("group", "dp"), None),
        P(("group", "dp"), None),
        P("dp", None),
        P(("group", "dp"), None, None),
        P(("group", "dp"), None, None),
        P(("group", "dp")),
        P("group"),
    )
    return jax.shard_map(
        body,
        mesh=mesh,
        in_specs=placed,
        out_specs=(
            P(("group", "dp"), None),
            P(("group", "dp"), None),
            P(("group", "dp"), None, None),
            P(("group", "dp"), None, None),
        ),
        check_vma=False,
    )
```

profile of v0, /device:TPU:1, one launch (start us, length us, event | category | flops | bytes accessed | tf_op | source)
XLA Modules:
  0.0 210.4 jit_solution(17078852605361177823)
XLA Ops:
  7.2 0.0 copy-start
  7.2 0.0 all-gather.2.cloned.1.call-start
  7.3 0.7 all-gather.2.cloned.1.call-update
  7.9 3.1 %constant_dynamic-update-slice_fusion.1 = bf16[8,16,8704]{2,1,0:T(8,128)(2,1)} fusion(bf16[8,16,8192]{2,1,0:T(8,128)(2,1)} %param.10), kind=kLoop, calls=%fused_computation.27 | loop fusion | bytes 4194304
  11.1 0.7 constant_dynamic-update-slice_fusion
  11.7 0.1 collective-permute-start.1
  11.8 2.5 %collective-permute-start = (bf16[8,16,8704]{2,1,0:T(8,128)(2,1)}, bf16[8,16,8704]{2,1,0:T(8,128)(2,1)}, u32[]{:S(2)}, u32[]{:S(2)}) collective-permute-start(bf16[8,16,8704]{2,1,0:T(8,128)(2,1)} %constant_dynamic-update-slice_fusion), channel_id=1, source_target_pairs={{0,1},{1,2},{2,3},{3,4},{4,5},{5,6},{6,7},{7,8},{8,9},{9,10},{10,1... | collective-permute-start | bytes 6684680 | tf_op jit(solution)/shard_map/ppermute | solution.py:14
  14.4 1.2 gather_fusion
  15.6 59.0 %collective-permute-done.1 = bf16[8,16,8704]{2,1,0:T(8,128)(2,1)} collective-permute-done((bf16[8,16,8704]{2,1,0:T(8,128)(2,1)}, bf16[8,16,8704]{2,1,0:T(8,128)(2,1)}, u32[]{:S(2)}, u32[]{:S(2)}) %collective-permute-start.1) | collective-permute-done | bytes 2228256 | tf_op jit(solution)/shard_map/ppermute | solution.py:16
  74.6 1.2 collective-permute-done
  75.9 3.9 %pad_maximum_fusion = bf16[24,16,8704]{2,1,0:T(8,128)(2,1)S(1)} fusion(bf16[8,16,8704]{2,1,0:T(8,128)(2,1)} %collective-permute-done.1, bf16[8,16,8704]{2,1,0:T(8,128)(2,1)} %constant_dynamic-update-slice_fusion, bf16[8,16,8704]{2,1,0:T(8,128)(2,1)} %collective-permute-done), kind=kLoop, calls=%fused_computation.9 | loop fusion | flops 6684672 | bytes 13369344 | tf_op jit(solution)/shard_map/concatenate | solution.py:12
  79.7 0.9 slice.44
  80.6 0.0 copy-start.4
  80.6 1.6 pad_maximum_fusion.2
  82.3 0.0 copy-done.4
  82.3 0.3 fusion.9
  82.6 1.8 fusion.8
  84.4 0.2 fusion.17
  84.7 1.8 fusion.16
  86.5 5.0 %fusion.2 = (f32[128,8704]{1,0:T(8,128)}, f32[128,8704]{1,0:T(8,128)}, f32[128,8704]{1,0:T(8,128)}) fusion(f32[384,8192]{1,0:T(8,128)S(1)} %fusion.16, f32[384,512]{1,0:T(8,128)S(1)} %fusion.17), kind=kLoop, calls=%fused_computation.10 | loop fusion | flops 3342336 | bytes 26738688 | tf_op jit(solution)/shard_map/concatenate | solution.py:73
  91.5 2.5 %collective-permute-start.2 = (f32[8,16,8704]{2,1,0:T(8,128)}, f32[8,16,8704]{2,1,0:T(8,128)S(1)}, u32[]{:S(2)}, u32[]{:S(2)}) collective-permute-start(f32[8,16,8704]{2,1,0:T(8,128)} %bitcast.39), channel_id=1, source_target_pairs={{0,1},{1,2},{2,3},{3,4},{4,5},{5,6},{6,7},{7,8},{8,9},{9,10},{10,1... | collective-permute-start | bytes 13369352 | tf_op jit(solution)/shard_map/ppermute | solution.py:14
  94.0 0.0 collective-permute-start.3
  94.0 0.2 fusion.6
  94.2 0.0 slice-start.1
  94.2 6.3 %fusion = f32[128,8192]{1,0:T(8,128)} fusion(bf16[128,384]{0,1:T(8,128)(2,1)S(1)} %fusion.9, bf16[384,8192]{1,0:T(8,128)(2,1)} %bitcast.34), kind=kOutput, calls=%fused_computation.7 | convolution fusion | flops 807403520 | bytes 10584064 | tf_op jit(solution)/shard_map/dot_general | solution.py:64
  100.5 89.3 %collective-permute-done.2 = f32[8,16,8704]{2,1,0:T(8,128)S(1)} collective-permute-done((f32[8,16,8704]{2,1,0:T(8,128)}, f32[8,16,8704]{2,1,0:T(8,128)S(1)}, u32[]{:S(2)}, u32[]{:S(2)}) %collective-permute-start.2) | collective-permute-done | bytes 4456480 | tf_op jit(solution)/shard_map/ppermute | solution.py:14
  189.8 0.0 collective-permute-done.3
  189.8 0.7 add_convert_fusion
  190.5 0.7 slice.50
  191.2 1.5 slice.49
  192.8 8.9 %fusion.1 = bf16[128,8192]{1,0:T(8,128)(2,1)} fusion(f32[128,8192]{1,0:T(8,128)} %fusion, bf16[128,512]{1,0:T(8,128)(2,1)S(1)} %copy-done.4, bf16[8192,512]{1,0:T(8,128)(2,1)} %all-gather.2.cloned.1.call-done), kind=kOutput, calls=%fused_computation.8 | convolution fusion | flops 1075838976 | bytes 14811136 | tf_op jit(solution)/shard_map/dot_general | solution.py:92
  201.6 1.9 fusion.4
  (20 shorter events, 0.1 us)
Async XLA Ops:
  7.2 75.4 %copy-start = (bf16[128,8192]{1,0:T(8,128)(2,1)S(1)}, bf16[128,8192]{1,0:T(8,128)(2,1)}, u32[]{:S(2)}) copy-start(bf16[128,8192]{1,0:T(8,128)(2,1)} %param.7) | copy-start | bytes 6291460
  7.2 3.9 %copy-start.5 = (bf16[8,16,512]{2,1,0:T(8,128)(2,1)S(1)}, bf16[8,16,512]{2,1,0:T(8,128)(2,1)}, u32[]{:S(2)}) copy-start(bf16[8,16,512]{2,1,0:T(8,128)(2,1)} %param.11) | copy-start | bytes 393220
  7.2 7.2 %copy-start.6 = (s32[128]{0:T(128)S(1)}, s32[128]{0:T(128)}, u32[]{:S(2)}) copy-start(s32[128]{0:T(128)} %param.12) | copy-start | bytes 1540
  7.2 7.2 %copy-start.1 = (s32[128]{0:T(128)S(1)}, s32[128]{0:T(128)}, u32[]{:S(2)}) copy-start(s32[128]{0:T(128)} %param.13) | copy-start | bytes 1540
  7.2 185.5 %all-gather.2.cloned.1.call-start = ((), (), s32[]{:S(2)}) async-start(), calls=%async_computation | async-start | bytes 8912896 | tf_op jit(solution)/shard_map/all_gather | solution.py:89
  11.7 62.9 %collective-permute-start.1 = (bf16[8,16,8704]{2,1,0:T(8,128)(2,1)}, bf16[8,16,8704]{2,1,0:T(8,128)(2,1)}, u32[]{:S(2)}, u32[]{:S(2)}) collective-permute-start(bf16[8,16,8704]{2,1,0:T(8,128)(2,1)} %constant_dynamic-update-slice_fusion), channel_id=1, source_target_pairs={{1,0},{2,1},{3,2},{4,3},{5,4},{6,5},{7,6},{8,7},{9,8},{10,9},{11,1... | collective-permute-start | bytes 6684680 | tf_op jit(solution)/shard_map/ppermute | solution.py:16
  11.8 64.1 %collective-permute-start = (bf16[8,16,8704]{2,1,0:T(8,128)(2,1)}, bf16[8,16,8704]{2,1,0:T(8,128)(2,1)}, u32[]{:S(2)}, u32[]{:S(2)}) collective-permute-start(bf16[8,16,8704]{2,1,0:T(8,128)(2,1)} %constant_dynamic-update-slice_fusion), channel_id=1, source_target_pairs={{0,1},{1,2},{2,3},{3,4},{4,5},{5,6},{6,7},{7,8},{8,9},{9,10},{10,1... | collective-permute-start | bytes 6684680 | tf_op jit(solution)/shard_map/ppermute | solution.py:14
  80.6 3.8 %copy-start.3 = (bf16[24,16,8192]{2,1,0:T(8,128)(2,1)}, bf16[24,16,8192]{2,1,0:T(8,128)(2,1)S(1)}, u32[]{:S(2)}) copy-start(bf16[24,16,8192]{2,1,0:T(8,128)(2,1)S(1)} %slice.44) | copy-start | bytes 18874372
  80.6 1.7 copy-start.4
  91.5 98.3 %collective-permute-start.2 = (f32[8,16,8704]{2,1,0:T(8,128)}, f32[8,16,8704]{2,1,0:T(8,128)S(1)}, u32[]{:S(2)}, u32[]{:S(2)}) collective-permute-start(f32[8,16,8704]{2,1,0:T(8,128)} %bitcast.39), channel_id=1, source_target_pairs={{0,1},{1,2},{2,3},{3,4},{4,5},{5,6},{6,7},{7,8},{8,9},{9,10},{10,1... | collective-permute-start | bytes 13369352 | tf_op jit(solution)/shard_map/ppermute | solution.py:14
  94.0 95.9 %collective-permute-start.3 = (f32[8,16,8704]{2,1,0:T(8,128)}, f32[8,16,8704]{2,1,0:T(8,128)S(1)}, u32[]{:S(2)}, u32[]{:S(2)}) collective-permute-start(f32[8,16,8704]{2,1,0:T(8,128)} %bitcast.38), channel_id=1, source_target_pairs={{1,0},{2,1},{3,2},{4,3},{5,4},{6,5},{7,6},{8,7},{9,8},{10,9},{11,1... | collective-permute-start | bytes 13369352 | tf_op jit(solution)/shard_map/ppermute | solution.py:16
  94.0 95.9 %slice-start = ((s8[4456448]{0:T(1024)(128)(4,1)}), s8[4194304]{0:T(1024)(128)(4,1)S(1)}, s32[]{:S(2)}) async-start(s8[4456448]{0:T(1024)(128)(4,1)} %bitcast.35), calls=%async_computation.1 | async-start | bytes 8388608
  94.2 95.6 %slice-start.1 = ((s8[4456448]{0:T(1024)(128)(4,1)}), s8[262144]{0:T(1024)(128)(4,1)S(1)}, s32[]{:S(2)}) async-start(s8[4456448]{0:T(1024)(128)(4,1)} %bitcast.35), calls=%async_computation.2 | async-start | bytes 524288
  192.7 8.9 %copy-start.2 = (bf16[8192,512]{1,0:T(8,128)(2,1)S(1)}, bf16[8192,512]{1,0:T(8,128)(2,1)}, u32[]{:S(2)}) copy-start(bf16[8192,512]{1,0:T(8,128)(2,1)} %all-gather.2.cloned.1.call-done) | copy-start | bytes 25165828
Sparse Core Ops, SparseCore 0:
  10.2 108.6 all-gather.1
where the time goes:
time: 211 us; the launch traced here: 210 us
  waiting for transfers between devices  150 us (71%)
  matrix products  21.4 us (10%)
  between operations  14.2 us (7%)
  other arithmetic  11.3 us (5%)
  local copies, waits for them, and re-layouts  8.17 us (4%)
  starting transfers between devices  5.12 us (2%)
    ppermute x2, waiting for transfers between devices, padded(): lax.ppermute(tail, axis, [(i, (i + 1) % count) for i in range(count)])  90.6 us
    ppermute x2, waiting for transfers between devices, padded(): lax.ppermute(head, axis, [((i + 1) % count, i) for i in range(count)])  59 us
    dot_general x1, matrix products, body(): lax.dot_general(output_cotangent, lax.all_gather(frozen_value_weight, 'dp...  8.88 us
    dot_general x1, matrix products, body(): jnp.dot(reverse_rank_rows, lowering_rows_flat, preferred_element_type=jnp...  6.28 us
    ppermute x2, starting transfers between devices, padded(): lax.ppermute(tail, axis, [(i, (i + 1) % count) for i in range(count)])  5.02 us
    concatenate x1, other arithmetic, body(): jnp.concatenate([down_terms, up_terms], axis=1)  5.01 us
  transfers between devices with their start and end apart: 5, of which 3 were waited for; matrix products, arithmetic and copies ran while one was open for 14% of the time, Pallas kernels for 0%

commit v1 on v0

v1 whole, which is shorter than its diff:
```python
import functools

import jax
import jax.numpy as jnp
from jax import lax
from jax.experimental import pallas as pl
from jax.experimental.pallas import tpu as pltpu
from jax.sharding import PartitionSpec as P

F32 = jnp.float32
BF16 = jnp.bfloat16
LAST = (((1,), (1,)), ((), ()))
FIRST = (((0,), (0,)), ((), ()))
TILE = 512


def dot(a, b, dims=None):
    if dims is None:
        return jnp.dot(a, b, preferred_element_type=F32)
    return lax.dot_general(a, b, dims, preferred_element_type=F32)


def kernel(
    planes, chips, tok, ct, w, low, rai, mask, sel,
    proj, tgrad, gdown, gup,
    full, near, packed, part, inc, req, acc,
    zs, zr, xs, xr, cs, cr, qs, qr, ps, pr, gs, gr,
):
    count = planes * chips * 2
    rows = w.shape[0]
    model = tok.shape[1]
    wide = near.shape[1]
    side = sel.shape[1]
    plane = chips * 2 * rows
    me = lax.axis_index("dp")
    core = lax.rem(me, 2)
    chip = lax.rem(me // 2, chips)
    level = me // (2 * chips)
    left, right = lax.rem(me + count - 1, count), lax.rem(me + 1, count)

    def at(z, x, c):
        return (lax.rem(z, planes) * chips + lax.rem(x, chips)) * 2 + c

    def block(owner):
        return full.at[pl.ds(pl.multiple_of(owner * rows, rows), rows)]

    def remote(src, dst, send, recv, device):
        copy = pltpu.make_async_remote_copy(
            src_ref=src, dst_ref=dst, send_sem=send, recv_sem=recv,
            device_id={"dp": device}, device_id_type=pl.DeviceIdType.MESH,
        )
        copy.start()
        return copy

    mates = [at(level, chip, 1 - core), left, right]
    mates += [at(level + dz, chip, core) for dz in range(1, planes)]
    mates += [at(level, chip + dx, core) for dx in range(1, chips)]
    barrier = pltpu.get_barrier_semaphore()
    for mate in mates:
        pl.semaphore_signal(
            barrier, inc=1, device_id={"dp": mate}, device_id_type=pl.DeviceIdType.MESH
        )
    pl.semaphore_wait(barrier, len(mates))

    sent = []
    ask = [
        remote(sel.at[0], req.at[1], qs.at[0], qr.at[0], left),
        remote(sel.at[2], req.at[0], qs.at[1], qr.at[1], right),
    ]
    across, beside, over = {}, {}, {}

    def spread_core(dz, dx):
        owner = at(level + planes - dz, chip + chips - dx, core)
        src = w if dz == 0 and dx == 0 else block(owner)
        n = dz * chips + dx
        over[dz, dx] = remote(src, block(owner), cs.at[n], cr.at[n], at(level, chip, 1 - core))

    def spread_chip(dz):
        owner = at(level + planes - dz, chip, core)
        src = w if dz == 0 else block(owner)
        for dx in range(1, chips):
            n = dz * (chips - 1) + dx - 1
            beside[dz, dx] = remote(
                src, block(owner), xs.at[n], xr.at[n], at(level, chip + dx, core)
            )

    order = sorted(range(1, planes), key=lambda d: min(d, planes - d))
    spread_chip(0)
    for dz in order:
        across[dz] = remote(
            w, block(me), zs.at[dz - 1], zr.at[dz - 1], at(level + dz, chip, core)
        )
    spread_core(0, 0)
    block(me)[...] = w[...]

    for s, (asked, device, slot) in enumerate(((1, left, 2), (0, right, 0))):
        ask[asked].wait_recv()

        @pl.loop(0, model // TILE)
        def _(i, s=s):
            cols = pl.ds(pl.multiple_of(i * TILE, TILE), TILE)
            packed[s, :, cols] = dot(req[s], low[:, cols]).astype(BF16)

        packed[s, :, pl.ds(model, wide - model)] = dot(req[s], rai[...]).astype(BF16)
        sent.append(
            remote(
                packed.at[s], near.at[pl.ds(slot * side, side)], ps.at[s], pr.at[s], device
            )
        )
    fetched = list(sent)

    @pl.loop(0, model // TILE)
    def _(i):
        cols = pl.ds(pl.multiple_of(i * TILE, TILE), TILE)
        near[pl.ds(side, side), cols] = dot(sel[1], low[:, cols]).astype(BF16)

    near[pl.ds(side, side), pl.ds(model, wide - model)] = dot(sel[1], rai[...]).astype(BF16)

    def arrive(dz):
        if dz:
            across[dz].wait_recv()
            spread_chip(dz)
            spread_core(dz, 0)

    if planes > 1:
        arrive(order[0])

    for copy in fetched:
        copy.wait_recv()

    def narrow_step(i, total):
        cols = pl.ds(pl.multiple_of(i * TILE, TILE), TILE)
        return total + dot(tok[:, cols], near[:, cols], LAST)

    narrow = lax.fori_loop(
        0, model // TILE, narrow_step, jnp.zeros((tok.shape[0], 3 * side), F32)
    )
    narrow = (narrow * mask[...]).astype(BF16)
    raising = near[:, pl.ds(model, wide - model)]
    back = (dot(ct[...], raising, LAST) * mask[...]).astype(BF16)

    @pl.loop(0, model // TILE)
    def _(i):
        cols = pl.ds(pl.multiple_of(i * TILE, TILE), TILE)
        terms = dot(back, tok[:, cols], FIRST).astype(BF16)
        part[0, :, cols] = terms[:side]
        part[1, :, cols] = terms[2 * side :]

    terms = dot(narrow, ct[...], FIRST).astype(BF16)
    part[0, :, pl.ds(model, wide - model)] = terms[:side]
    part[1, :, pl.ds(model, wide - model)] = terms[2 * side :]
    back_terms = [
        remote(part.at[0], inc.at[1], gs.at[0], gr.at[0], left),
        remote(part.at[1], inc.at[0], gs.at[1], gr.at[1], right),
    ]

    def use(dz):
        for dx in range(1, chips):
            beside[dz, dx].wait_recv()
            spread_core(dz, dx)

    def finish(dz):
        for dx in range(chips):
            over[dz, dx].wait_recv()
        start = lax.rem(level + planes - dz, planes) * plane

        @pl.loop(0, plane // TILE)
        def _(i):
            span = pl.ds(pl.multiple_of(start + i * TILE, TILE), TILE)
            held = full[span, :]
            acc[...] += dot(tok[:, span], held)
            lora = dot(back, near[:, span]).astype(BF16).astype(F32)
            tgrad[:, span] = (dot(ct[...], held, LAST) + lora).astype(BF16)

    acc[...] = jnp.zeros_like(acc)
    use(0)
    for dz in order[1:]:
        arrive(dz)
    finish(0)
    for dz in order:
        use(dz)
        if dz == order[-1]:
            for copy in back_terms:
                copy.wait_recv()
            own_back = dot(back[:, side : 2 * side], sel[1]).astype(BF16)
            own_narrow = dot(narrow[:, side : 2 * side], sel[1]).astype(BF16)

            @pl.loop(0, model // TILE)
            def _(i):
                cols = pl.ds(pl.multiple_of(i * TILE, TILE), TILE)
                gdown[:, cols] = (
                    dot(own_back, tok[:, cols], FIRST)
                    + dot(req[0], inc[0, :, cols], FIRST)
                    + dot(req[1], inc[1, :, cols], FIRST)
                ).astype(BF16)

            tail = pl.ds(model, wide - model)
            gup[...] = (
                dot(own_narrow, ct[...], FIRST)
                + dot(req[0], inc[0, :, tail], FIRST)
                + dot(req[1], inc[1, :, tail], FIRST)
            ).astype(BF16)
        finish(dz)
    proj[...] = (acc[...] + dot(narrow, raising).astype(BF16).astype(F32)).astype(BF16)

    for copy in (
        ask + sent + back_terms + list(across.values()) + list(beside.values())
        + list(over.values())
    ):
        copy.wait_send()


def body(tokens, output_cotangent, weight, lowering, raising, tenant, tenant_row_index):
    count = lax.axis_size("dp")
    here = lax.axis_index("dp")
    chips = 2 if count < 64 else 4
    planes = count // (2 * chips)
    token_count, model = tokens.shape
    value = output_cotangent.shape[1]
    stored, rank = lowering.shape[:2]
    ranks = stored * rank
    row = jnp.take(tenant_row_index, tenant)
    owner = row // stored
    side = (owner - here + 1 + count) % count
    local = row % stored
    on = side[:, None] == jnp.arange(3)[None, :]
    lo = jnp.min(jnp.where(on, local[:, None], stored - 1), axis=0)
    hi = jnp.max(jnp.where(on, local[:, None], 0), axis=0)
    slots = jnp.stack([lo, hi], axis=1)
    hit = on[:, :, None] & (local[:, None, None] == slots[None])
    first = hit[:, :, :1]
    hit = jnp.concatenate([first, hit[:, :, 1:] & ~first], axis=2)
    mask = jnp.broadcast_to(
        hit.reshape(token_count, 6, 1), (token_count, 6, rank)
    ).reshape(token_count, 6 * rank).astype(F32)
    wanted = slots[:, :, None] * rank + jnp.arange(rank)[None, None, :]
    sel = (
        wanted.reshape(3, 2 * rank, 1) == jnp.arange(ranks)[None, None, :]
    ).astype(BF16)
    wide = model + value
    dma = pltpu.SemaphoreType.DMA
    vmem = pl.BlockSpec(memory_space=pltpu.VMEM)
    proj, tgrad, gdown, gup = pl.pallas_call(
        functools.partial(kernel, planes, chips),
        out_shape=(
            jax.ShapeDtypeStruct((token_count, value), BF16),
            jax.ShapeDtypeStruct((token_count, model), BF16),
            jax.ShapeDtypeStruct((ranks, model), BF16),
            jax.ShapeDtypeStruct((ranks, value), BF16),
        ),
        in_specs=[vmem] * 7,
        out_specs=(vmem,) * 4,
        scratch_shapes=[
            pltpu.VMEM((model, value), BF16),
            pltpu.VMEM((6 * rank, wide), BF16),
            pltpu.VMEM((2, 2 * rank, wide), BF16),
            pltpu.VMEM((2, 2 * rank, wide), BF16),
            pltpu.VMEM((2, 2 * rank, wide), BF16),
            pltpu.VMEM((2, 2 * rank, ranks), BF16),
            pltpu.VMEM((token_count, value), F32),
            dma((planes,)), dma((planes,)),
            dma((planes * chips,)), dma((planes * chips,)),
            dma((planes * chips,)), dma((planes * chips,)),
            dma((2,)), dma((2,)), dma((2,)), dma((2,)), dma((2,)), dma((2,)),
        ],
        compiler_params=pltpu.CompilerParams(
            collective_id=0, has_side_effects=True, vmem_limit_bytes=48 * 1024 * 1024
        ),
        cost_estimate=pl.CostEstimate(
            flops=4 * token_count * model * value,
            bytes_accessed=8 * token_count * model,
            transcendentals=0,
        ),
    )(
        tokens, output_cotangent, weight,
        lowering.reshape(ranks, model), raising.reshape(ranks, value), mask, sel,
    )
    return (
        proj, tgrad,
        gdown.reshape(stored, rank, model), gup.reshape(stored, rank, value),
    )


def solution(mesh):
    rows = P(("group", "dp"), None)
    stacks = P(("group", "dp"), None, None)
    return jax.shard_map(
        body,
        mesh=mesh,
        in_specs=(rows, rows, P("dp", None), stacks, stacks, P(("group", "dp")), P("group")),
        out_specs=(rows, rows, stacks, stacks),
        check_vma=False,
    )
```

time: 211 us -> 109 us (0.52)
  the two profiles are of different devices: /device:TPU:1 before, /device:TPU:20 now
where the time goes in v1:
time: 109 us
  Pallas kernels  97 us (89%)
  local copies, waits for them, and re-layouts  8.56 us (8%)
  other arithmetic  2.37 us (2%)
    pallas_call x1, Pallas kernels, body(): pl.pallas_call(functools.partial(kernel, planes, chips), out_shape=(jax.S...  97 us
    unnamed x12, local copies, waits for them, and re-layouts  6.81 us

profile of v1, /device:TPU:20, one launch (start us, length us, event | category | flops | bytes accessed | tf_op | source)
XLA Modules:
  0.0 108.6 jit_solution(17012626420533975018)
XLA Ops:
  0.6 0.0 copy-start
  0.6 0.7 compare_select_fusion
  1.3 0.1 add.71
  1.4 0.0 copy-done
  1.4 1.2 %gather_fusion = s32[128]{0:T(128)S(1)} fusion(s32[128]{0:T(128)S(1)} %copy-done, s32[1024]{0:T(1024)S(1)} %pad_clamp_fusion), kind=kCustom, calls=%fused_computation | custom fusion | bytes 1536 | tf_op jit(solution)/shard_map/jit(_take)/gather | solution.py:222
  2.6 0.7 and_select_fusion
  3.3 0.7 and_select_fusion.1
  4.0 0.1 select_reduce_fusion.1
  4.2 0.1 copy.14
  4.3 0.1 add.68
  4.3 0.1 add.69
  4.4 0.1 copy.13
  4.5 0.1 compare_and_fusion
  4.6 0.1 fusion.sel
  4.7 0.1 copy.15.mask
  4.8 0.0 copy-start.1
  4.8 1.0 copy-done.1
  5.9 0.0 copy-start.2
  5.9 0.9 copy-done.2
  6.8 0.0 copy-start.3
  6.8 0.9 copy-done.3
  7.7 97.0 %shard_map.102 = (bf16[128,512]{1,0:T(8,128)(2,1)S(1)}, bf16[128,8192]{1,0:T(8,128)(2,1)S(1)}, bf16[128,8192]{1,0:T(8,128)(2,1)S(1)}, bf16[128,512]{1,0:T(8,128)(2,1)S(1)}) custom-call(bf16[128,8192]{1,0:T(8,128)(2,1)} %tok.1, bf16[128,512]{1,0:T(8,128)(2,1)S(1)} %copy-done.2, bf16[512,512]{1,0:T(8,128)(2,1)S(1)} %copy-done.1, bf16[128,8192]{1,0:T(8,128)(2,1)} %bitcast.15, ...), custom_call_target="tpu_custom_call" | custom-call | flops 2147483648 | bytes 8388608 | tf_op jit(solution)/shard_map/pallas_call | solution.py:243
  104.7 0.7 copy.20
  105.3 1.3 %copy.21 = bf16[128,8192]{1,0:T(8,128)(2,1)} copy(bf16[128,8192]{1,0:T(8,128)(2,1)S(1)} %get-tuple-element.25) | data formatting | bytes 4194304
  106.7 1.3 %copy.22 = bf16[8,16,8192]{2,1,0:T(8,128)(2,1)} copy(bf16[8,16,8192]{2,1,0:T(8,128)(2,1)S(1)} %bitcast.9) | data formatting | bytes 4194304
  108.0 0.7 copy.23
  (9 shorter events, 0.1 us)
Async XLA Ops:
  0.6 0.8 copy-start
  4.8 1.0 copy-start.1
  5.9 0.9 copy-start.2
  6.8 0.9 copy-start.3

commit v2 on v1

--- a/solution.py
+++ b/solution.py
@@ -24,7 +24,7 @@
     planes, chips, tok, ct, w, low, rai, mask, sel,
     proj, tgrad, gdown, gup,
     full, near, packed, part, inc, req, acc,
-    zs, zr, xs, xr, cs, cr, qs, qr, ps, pr, gs, gr,
+    zs, zr, xs, xr, ys, yr, cs, cr, qs, qr, ps, pr, gs, gr,
 ):
     count = planes * chips * 2
     rows = w.shape[0]
@@ -38,27 +38,36 @@
     level = me // (2 * chips)
     left, right = lax.rem(me + count - 1, count), lax.rem(me + 1, count)
 
+    half = rows // 2
+    group = lax.axis_index("group")
+    mine, other = group, 1 - group
+
     def at(z, x, c):
         return (lax.rem(z, planes) * chips + lax.rem(x, chips)) * 2 + c
 
     def block(owner):
         return full.at[pl.ds(pl.multiple_of(owner * rows, rows), rows)]
 
-    def remote(src, dst, send, recv, device):
+    def piece(owner, part_of):
+        return full.at[pl.ds(pl.multiple_of(owner * rows + part_of * half, half), half)]
+
+    def remote(src, dst, send, recv, device, to_group=None):
         copy = pltpu.make_async_remote_copy(
             src_ref=src, dst_ref=dst, send_sem=send, recv_sem=recv,
-            device_id={"dp": device}, device_id_type=pl.DeviceIdType.MESH,
+            device_id={"group": group if to_group is None else to_group, "dp": device},
+            device_id_type=pl.DeviceIdType.MESH,
         )
         copy.start()
         return copy
 
-    mates = [at(level, chip, 1 - core), left, right]
-    mates += [at(level + dz, chip, core) for dz in range(1, planes)]
-    mates += [at(level, chip + dx, core) for dx in range(1, chips)]
+    mates = [(group, at(level, chip, 1 - core)), (group, left), (group, right), (other, me)]
+    mates += [(group, at(level + dz, chip, core)) for dz in range(1, planes)]
+    mates += [(group, at(level, chip + dx, core)) for dx in range(1, chips)]
     barrier = pltpu.get_barrier_semaphore()
-    for mate in mates:
+    for to_group, mate in mates:
         pl.semaphore_signal(
-            barrier, inc=1, device_id={"dp": mate}, device_id_type=pl.DeviceIdType.MESH
+            barrier, inc=1, device_id={"group": to_group, "dp": mate},
+            device_id_type=pl.DeviceIdType.MESH,
         )
     pl.semaphore_wait(barrier, len(mates))
 
@@ -67,30 +76,41 @@
         remote(sel.at[0], req.at[1], qs.at[0], qr.at[0], left),
         remote(sel.at[2], req.at[0], qs.at[1], qr.at[1], right),
     ]
-    across, beside, over = {}, {}, {}
-
-    def spread_core(dz, dx):
-        owner = at(level + planes - dz, chip + chips - dx, core)
-        src = w if dz == 0 and dx == 0 else block(owner)
-        n = dz * chips + dx
-        over[dz, dx] = remote(src, block(owner), cs.at[n], cr.at[n], at(level, chip, 1 - core))
-
-    def spread_chip(dz):
-        owner = at(level + planes - dz, chip, core)
-        src = w if dz == 0 else block(owner)
+    across, beside, facing, over = {}, {}, {}, {}
+    order = sorted(range(1, planes), key=lambda d: min(d, planes - d))
+    last = order[-1]
+
+    def source(dz, dx):
+        return at(level + planes - dz, chip + chips - dx, core)
+
+    def to_core(dz, dx, which):
+        if dz == 0:
+            dst = block(source(0, dx))
+            src, n = (dst if dx else w), dx
+        else:
+            src = dst = piece(source(dz, dx), other if which else mine)
+            n = chips + ((dz - 1) * chips + dx) * 2 + which
+        over[dz, dx, which] = remote(
+            src, dst, cs.at[n], cr.at[n], at(level, chip, 1 - core)
+        )
+
+    def to_chip(key, src, dst, first):
         for dx in range(1, chips):
-            n = dz * (chips - 1) + dx - 1
-            beside[dz, dx] = remote(
-                src, block(owner), xs.at[n], xr.at[n], at(level, chip + dx, core)
-            )
-
-    order = sorted(range(1, planes), key=lambda d: min(d, planes - d))
-    spread_chip(0)
+            n = first * (chips - 1) + dx - 1
+            beside[key, dx] = remote(src, dst, xs.at[n], xr.at[n], at(level, chip + dx, core))
+
+    def to_group(dz, dx):
+        ref = piece(source(dz, dx), mine)
+        n = (dz - 1) * chips + dx
+        facing[dz, dx] = remote(ref, ref, ys.at[n], yr.at[n], me, other)
+
     for dz in order:
         across[dz] = remote(
-            w, block(me), zs.at[dz - 1], zr.at[dz - 1], at(level + dz, chip, core)
-        )
-    spread_core(0, 0)
+            w.at[pl.ds(pl.multiple_of(mine * half, half), half)], piece(me, mine),
+            zs.at[dz - 1], zr.at[dz - 1], at(level + dz, chip, core),
+        )
+    to_chip("own", w, block(me), 0)
+    to_core(0, 0, 0)
     block(me)[...] = w[...]
 
     for s, (asked, device, slot) in enumerate(((1, left, 2), (0, right, 0))):
@@ -116,14 +136,41 @@
 
     near[pl.ds(side, side), pl.ds(model, wide - model)] = dot(sel[1], rai[...]).astype(BF16)
 
-    def arrive(dz):
-        if dz:
-            across[dz].wait_recv()
-            spread_chip(dz)
-            spread_core(dz, 0)
-
-    if planes > 1:
-        arrive(order[0])
+    def from_level(dz):
+        across[dz].wait_recv()
+        ref = piece(source(dz, 0), mine)
+        to_group(dz, 0)
+        to_chip(dz, ref, ref, dz)
+        to_core(dz, 0, 0)
+
+    def own_chip():
+        for dx in range(1, chips):
+            beside["own", dx].wait_recv()
+            to_core(0, dx, 0)
+
+    def from_chip(dz):
+        for dx in range(1, chips):
+            beside[dz, dx].wait_recv()
+            if dz != last:
+                to_group(dz, dx)
+            to_core(dz, dx, 0)
+
+    def from_group(dz):
+        facing[dz, 0].wait_recv()
+        if dz == last:
+            ref = piece(source(dz, 0), other)
+            to_chip("last", ref, ref, planes)
+        to_core(dz, 0, 1)
+
+    def from_corner(dz):
+        for dx in range(1, chips):
+            (beside["last", dx] if dz == last else facing[dz, dx]).wait_recv()
+            to_core(dz, dx, 1)
+
+    from_level(order[0])
+    own_chip()
+    for dz in order[1:-1]:
+        from_level(dz)
 
     for copy in fetched:
         copy.wait_recv()
@@ -154,14 +201,10 @@
         remote(part.at[1], inc.at[0], gs.at[1], gr.at[1], right),
     ]
 
-    def use(dz):
-        for dx in range(1, chips):
-            beside[dz, dx].wait_recv()
-            spread_core(dz, dx)
-
     def finish(dz):
         for dx in range(chips):
-            over[dz, dx].wait_recv()
+            for which in range(2 if dz else 1):
+                over[dz, dx, which].wait_recv()
         start = lax.rem(level + planes - dz, planes) * plane
 
         @pl.loop(0, plane // TILE)
@@ -173,13 +216,20 @@
             tgrad[:, span] = (dot(ct[...], held, LAST) + lora).astype(BF16)
 
     acc[...] = jnp.zeros_like(acc)
-    use(0)
-    for dz in order[1:]:
-        arrive(dz)
+    from_chip(order[0])
+    from_group(order[0])
     finish(0)
+    if last != order[0]:
+        from_level(last)
+    for dz in order[1:-1]:
+        from_chip(dz)
+        from_group(dz)
+    if last != order[0]:
+        from_chip(last)
+        from_group(last)
     for dz in order:
-        use(dz)
-        if dz == order[-1]:
+        from_corner(dz)
+        if dz == last:
             for copy in back_terms:
                 copy.wait_recv()
             own_back = dot(back[:, side : 2 * side], sel[1]).astype(BF16)
@@ -205,7 +255,7 @@
 
     for copy in (
         ask + sent + back_terms + list(across.values()) + list(beside.values())
-        + list(over.values())
+        + list(facing.values()) + list(over.values())
     ):
         copy.wait_send()
 
@@ -259,8 +309,9 @@
             pltpu.VMEM((2, 2 * rank, ranks), BF16),
             pltpu.VMEM((token_count, value), F32),
             dma((planes,)), dma((planes,)),
+            dma(((planes + 1) * chips,)), dma(((planes + 1) * chips,)),
             dma((planes * chips,)), dma((planes * chips,)),
-            dma((planes * chips,)), dma((planes * chips,)),
+            dma((2 * planes * chips,)), dma((2 * planes * chips,)),
             dma((2,)), dma((2,)), dma((2,)), dma((2,)), dma((2,)), dma((2,)),
         ],
         compiler_params=pltpu.CompilerParams(

time: 109 us -> 90.6 us (0.83)
  the two profiles are of different devices: /device:TPU:20 before, /device:TPU:15 now
where the time goes in v2:
time: 90.6 us; the launch traced here: 90.3 us
  Pallas kernels  78.7 us (87%)
  local copies, waits for them, and re-layouts  8.56 us (9%)
  other arithmetic  2.37 us (3%)
    pallas_call x1, Pallas kernels, body(): pl.pallas_call(functools.partial(kernel, planes, chips), out_shape=(jax.S...  78.7 us
    unnamed x12, local copies, waits for them, and re-layouts  6.81 us

profile of v2, /device:TPU:15, one launch (start us, length us, event | category | flops | bytes accessed | tf_op | source)
XLA Modules:
  0.0 90.3 jit_solution(7035838404271404723)
XLA Ops:
  0.6 0.0 copy-start
  0.6 0.7 compare_select_fusion
  1.3 0.1 add.71
  1.4 0.0 copy-done
  1.4 1.2 %gather_fusion = s32[128]{0:T(128)S(1)} fusion(s32[128]{0:T(128)S(1)} %copy-done, s32[1024]{0:T(1024)S(1)} %pad_clamp_fusion), kind=kCustom, calls=%fused_computation | custom fusion | bytes 1536 | tf_op jit(solution)/shard_map/jit(_take)/gather | solution.py:272
  2.6 0.7 and_select_fusion
  3.3 0.7 and_select_fusion.1
  4.0 0.1 select_reduce_fusion.1
  4.2 0.1 copy.14
  4.3 0.1 add.68
  4.3 0.1 add.69
  4.4 0.1 copy.13
  4.5 0.1 compare_and_fusion
  4.6 0.1 fusion.sel
  4.7 0.1 copy.15.mask
  4.8 0.0 copy-start.1
  4.8 1.0 %copy-done.1 = bf16[512,512]{1,0:T(8,128)(2,1)S(1)} copy-done((bf16[512,512]{1,0:T(8,128)(2,1)S(1)}, bf16[512,512]{1,0:T(8,128)(2,1)}, u32[]{:S(2)}) %copy-start.1) | copy-done | bytes 524312
  5.9 0.0 copy-start.2
  5.9 0.9 copy-done.2
  6.8 0.0 copy-start.3
  6.8 0.9 copy-done.3
  7.7 78.7 %shard_map.102 = (bf16[128,512]{1,0:T(8,128)(2,1)S(1)}, bf16[128,8192]{1,0:T(8,128)(2,1)S(1)}, bf16[128,8192]{1,0:T(8,128)(2,1)S(1)}, bf16[128,512]{1,0:T(8,128)(2,1)S(1)}) custom-call(bf16[128,8192]{1,0:T(8,128)(2,1)} %tok.1, bf16[128,512]{1,0:T(8,128)(2,1)S(1)} %copy-done.2, bf16[512,512]{1,0:T(8,128)(2,1)S(1)} %copy-done.1, bf16[128,8192]{1,0:T(8,128)(2,1)} %bitcast.15, ...), custom_call_target="tpu_custom_call" | custom-call | flops 2147483648 | bytes 8388608 | tf_op jit(solution)/shard_map/pallas_call | solution.py:293
  86.4 0.7 copy.20
  87.0 1.3 %copy.21 = bf16[128,8192]{1,0:T(8,128)(2,1)} copy(bf16[128,8192]{1,0:T(8,128)(2,1)S(1)} %get-tuple-element.25) | data formatting | bytes 4194304
  88.4 1.3 %copy.22 = bf16[8,16,8192]{2,1,0:T(8,128)(2,1)} copy(bf16[8,16,8192]{2,1,0:T(8,128)(2,1)S(1)} %bitcast.9) | data formatting | bytes 4194304
  89.7 0.7 copy.23
  (9 shorter events, 0.1 us)
Async XLA Ops:
  0.6 0.8 copy-start
  4.8 1.0 %copy-start.1 = (bf16[512,512]{1,0:T(8,128)(2,1)S(1)}, bf16[512,512]{1,0:T(8,128)(2,1)}, u32[]{:S(2)}) copy-start(bf16[512,512]{1,0:T(8,128)(2,1)} %w.1) | copy-start | bytes 1572868
  5.9 0.9 %copy-start.2 = (bf16[128,512]{1,0:T(8,128)(2,1)S(1)}, bf16[128,512]{1,0:T(8,128)(2,1)}, u32[]{:S(2)}) copy-start(bf16[128,512]{1,0:T(8,128)(2,1)} %ct.1) | copy-start | bytes 393220
  6.8 0.9 %copy-start.3 = (bf16[8,16,512]{2,1,0:T(8,128)(2,1)S(1)}, bf16[8,16,512]{2,1,0:T(8,128)(2,1)}, u32[]{:S(2)}) copy-start(bf16[8,16,512]{2,1,0:T(8,128)(2,1)} %param.11) | copy-start | bytes 393220

commit v3 on v2

--- a/solution.py
+++ b/solution.py
@@ -11,7 +11,7 @@
 BF16 = jnp.bfloat16
 LAST = (((1,), (1,)), ((), ()))
 FIRST = (((0,), (0,)), ((), ()))
-TILE = 512
+TILE = 2048
 
 
 def dot(a, b, dims=None):
@@ -84,12 +84,11 @@
         return at(level + planes - dz, chip + chips - dx, core)
 
     def to_core(dz, dx, which):
-        if dz == 0:
-            dst = block(source(0, dx))
-            src, n = (dst if dx else w), dx
+        if dz == 0 and dx == 0:
+            src, dst = w, block(me)
         else:
             src = dst = piece(source(dz, dx), other if which else mine)
-            n = chips + ((dz - 1) * chips + dx) * 2 + which
+        n = (dz * chips + dx) * 2 + which
         over[dz, dx, which] = remote(
             src, dst, cs.at[n], cr.at[n], at(level, chip, 1 - core)
         )
@@ -101,7 +100,7 @@
 
     def to_group(dz, dx):
         ref = piece(source(dz, dx), mine)
-        n = (dz - 1) * chips + dx
+        n = dz * chips + dx
         facing[dz, dx] = remote(ref, ref, ys.at[n], yr.at[n], me, other)
 
     for dz in order:
@@ -109,7 +108,7 @@
             w.at[pl.ds(pl.multiple_of(mine * half, half), half)], piece(me, mine),
             zs.at[dz - 1], zr.at[dz - 1], at(level + dz, chip, core),
         )
-    to_chip("own", w, block(me), 0)
+    to_chip(0, w.at[pl.ds(pl.multiple_of(mine * half, half), half)], piece(me, mine), 0)
     to_core(0, 0, 0)
     block(me)[...] = w[...]
 
@@ -143,32 +142,23 @@
         to_chip(dz, ref, ref, dz)
         to_core(dz, 0, 0)
 
-    def own_chip():
-        for dx in range(1, chips):
-            beside["own", dx].wait_recv()
-            to_core(0, dx, 0)
-
     def from_chip(dz):
         for dx in range(1, chips):
             beside[dz, dx].wait_recv()
-            if dz != last:
-                to_group(dz, dx)
+            to_group(dz, dx)
             to_core(dz, dx, 0)
 
     def from_group(dz):
         facing[dz, 0].wait_recv()
-        if dz == last:
-            ref = piece(source(dz, 0), other)
-            to_chip("last", ref, ref, planes)
         to_core(dz, 0, 1)
 
     def from_corner(dz):
         for dx in range(1, chips):
-            (beside["last", dx] if dz == last else facing[dz, dx]).wait_recv()
+            facing[dz, dx].wait_recv()
             to_core(dz, dx, 1)
 
+    from_chip(0)
     from_level(order[0])
-    own_chip()
     for dz in order[1:-1]:
         from_level(dz)
 
@@ -203,13 +193,14 @@
 
     def finish(dz):
         for dx in range(chips):
-            for which in range(2 if dz else 1):
+            for which in range(2 if dz or dx else 1):
                 over[dz, dx, which].wait_recv()
         start = lax.rem(level + planes - dz, planes) * plane
-
-        @pl.loop(0, plane // TILE)
+        step = min(plane, TILE)
+
+        @pl.loop(0, plane // step)
         def _(i):
-            span = pl.ds(pl.multiple_of(start + i * TILE, TILE), TILE)
+            span = pl.ds(pl.multiple_of(start + i * step, step), step)
             held = full[span, :]
             acc[...] += dot(tok[:, span], held)
             lora = dot(back, near[:, span]).astype(BF16).astype(F32)
@@ -218,17 +209,20 @@
     acc[...] = jnp.zeros_like(acc)
     from_chip(order[0])
     from_group(order[0])
-    finish(0)
+    from_corner(0)
     if last != order[0]:
         from_level(last)
+    finish(0)
     for dz in order[1:-1]:
         from_chip(dz)
         from_group(dz)
+    from_corner(order[0])
     if last != order[0]:
         from_chip(last)
         from_group(last)
     for dz in order:
-        from_corner(dz)
+        if dz != order[0]:
+            from_corner(dz)
         if dz == last:
             for copy in back_terms:
                 copy.wait_recv()

time: 90.6 us -> 79.8 us (0.88)
  the two profiles are of different devices: /device:TPU:15 before, /device:TPU:19 now
where the time goes in v3:
time: 79.8 us; the launch traced here: 79.6 us
  Pallas kernels  67.9 us (85%)
  local copies, waits for them, and re-layouts  8.56 us (11%)
  other arithmetic  2.37 us (3%)
    pallas_call x1, Pallas kernels, body(): pl.pallas_call(functools.partial(kernel, planes, chips), out_shape=(jax.S...  67.9 us
    unnamed x12, local copies, waits for them, and re-layouts  6.81 us

profile of v3, /device:TPU:19, one launch (start us, length us, event | category | flops | bytes accessed | tf_op | source)
XLA Modules:
  0.0 79.6 jit_solution(7118580496942239867)
XLA Ops:
  0.6 0.0 copy-start
  0.6 0.7 compare_select_fusion
  1.3 0.1 add.71
  1.4 0.0 copy-done
  1.4 1.2 %gather_fusion = s32[128]{0:T(128)S(1)} fusion(s32[128]{0:T(128)S(1)} %copy-done, s32[1024]{0:T(1024)S(1)} %pad_clamp_fusion), kind=kCustom, calls=%fused_computation | custom fusion | bytes 1536 | tf_op jit(solution)/shard_map/jit(_take)/gather | solution.py:266
  2.6 0.7 and_select_fusion
  3.3 0.7 and_select_fusion.1
  4.0 0.1 select_reduce_fusion.1
  4.2 0.1 copy.14
  4.3 0.1 add.68
  4.3 0.1 add.69
  4.4 0.1 copy.13
  4.5 0.1 compare_and_fusion
  4.6 0.1 fusion.sel
  4.7 0.1 copy.15.mask
  4.8 0.0 copy-start.1
  4.8 1.0 %copy-done.1 = bf16[512,512]{1,0:T(8,128)(2,1)S(1)} copy-done((bf16[512,512]{1,0:T(8,128)(2,1)S(1)}, bf16[512,512]{1,0:T(8,128)(2,1)}, u32[]{:S(2)}) %copy-start.1) | copy-done | bytes 524312
  5.9 0.0 copy-start.2
  5.9 0.9 %copy-done.2 = bf16[128,512]{1,0:T(8,128)(2,1)S(1)} copy-done((bf16[128,512]{1,0:T(8,128)(2,1)S(1)}, bf16[128,512]{1,0:T(8,128)(2,1)}, u32[]{:S(2)}) %copy-start.2) | copy-done | bytes 131096
  6.8 0.0 copy-start.3
  6.8 0.9 %copy-done.3 = bf16[8,16,512]{2,1,0:T(8,128)(2,1)S(1)} copy-done((bf16[8,16,512]{2,1,0:T(8,128)(2,1)S(1)}, bf16[8,16,512]{2,1,0:T(8,128)(2,1)}, u32[]{:S(2)}) %copy-start.3) | copy-done | bytes 131096
  7.7 67.9 %shard_map.102 = (bf16[128,512]{1,0:T(8,128)(2,1)S(1)}, bf16[128,8192]{1,0:T(8,128)(2,1)S(1)}, bf16[128,8192]{1,0:T(8,128)(2,1)S(1)}, bf16[128,512]{1,0:T(8,128)(2,1)S(1)}) custom-call(bf16[128,8192]{1,0:T(8,128)(2,1)} %tok.1, bf16[128,512]{1,0:T(8,128)(2,1)S(1)} %copy-done.2, bf16[512,512]{1,0:T(8,128)(2,1)S(1)} %copy-done.1, bf16[128,8192]{1,0:T(8,128)(2,1)} %bitcast.15, ...), custom_call_target="tpu_custom_call" | custom-call | flops 2147483648 | bytes 8388608 | tf_op jit(solution)/shard_map/pallas_call | solution.py:287
  75.6 0.7 copy.20
  76.3 1.3 %copy.21 = bf16[128,8192]{1,0:T(8,128)(2,1)} copy(bf16[128,8192]{1,0:T(8,128)(2,1)S(1)} %get-tuple-element.25) | data formatting | bytes 4194304
  77.6 1.3 %copy.22 = bf16[8,16,8192]{2,1,0:T(8,128)(2,1)} copy(bf16[8,16,8192]{2,1,0:T(8,128)(2,1)S(1)} %bitcast.9) | data formatting | bytes 4194304
  78.9 0.7 copy.23
  (9 shorter events, 0.1 us)
Async XLA Ops:
  0.6 0.8 copy-start
  4.8 1.0 %copy-start.1 = (bf16[512,512]{1,0:T(8,128)(2,1)S(1)}, bf16[512,512]{1,0:T(8,128)(2,1)}, u32[]{:S(2)}) copy-start(bf16[512,512]{1,0:T(8,128)(2,1)} %w.1) | copy-start | bytes 1572868
  5.9 0.9 %copy-start.2 = (bf16[128,512]{1,0:T(8,128)(2,1)S(1)}, bf16[128,512]{1,0:T(8,128)(2,1)}, u32[]{:S(2)}) copy-start(bf16[128,512]{1,0:T(8,128)(2,1)} %ct.1) | copy-start | bytes 393220
  6.8 0.9 %copy-start.3 = (bf16[8,16,512]{2,1,0:T(8,128)(2,1)S(1)}, bf16[8,16,512]{2,1,0:T(8,128)(2,1)}, u32[]{:S(2)}) copy-start(bf16[8,16,512]{2,1,0:T(8,128)(2,1)} %param.11) | copy-start | bytes 393220
